TPU v7x, 128 devices: a whole 4x4x4 slice. The times are simulated.
128 devices in a mesh: depth: 8 (over z, core), row: 16 (over y, x).
Axes of the slice: x: 4, y: 4, z: 4, core: 2. Of those that a mesh axis runs over, the one named last changes fastest.
Arguments:
- volume: float32 [384, 1024, 2048], P('depth', 'row'), may hold values from -6 to 6
- transfer: float32 [8], replicated, may hold values from 0.3 to 1.2
Outputs:
- image: float32 [4, 1024, 2048], P(None, 'row', 'depth')
All inputs are finite; a program needn't handle non-finite values.
Results may differ from a plain program's by a relative error of at most 0.0003.
Values sent between devices are 32-bit elements; how exact they have to be, the bound alone decides.
A program may use at most 192 MiB of HBM per device.

v0:
```python
import jax
import jax.numpy as jnp
from jax import lax
from jax.sharding import PartitionSpec as P


def with_halo(cells, sides, width):
    for axis, dim in sides:
        count = lax.axis_size(axis)
        ends = count - 1
        head = lax.slice_in_dim(cells, 0, width, axis=dim)
        tail = lax.slice_in_dim(cells, cells.shape[dim] - width, cells.shape[dim], axis=dim)
        cells = jnp.concatenate(
            [
                lax.ppermute(tail, axis, [(i, (i + 1) % count) for i in range(ends)]),
                cells,
                lax.ppermute(head, axis, [((i + 1) % count, i) for i in range(ends)]),
            ],
            axis=dim,
        )
    return cells


def slope_cols(center):
    zero_col = jnp.zeros_like(center[..., :1])
    right = jnp.concatenate([center[..., 1:], zero_col], -1)
    left = jnp.concatenate([zero_col, center[..., :-1]], -1)
    return 0.5 * (right - left)


def emit(framed, transfer, slices):
    center = framed[1:-1, 1:-1, :]
    slope_depth = 0.5 * (framed[2:, 1:-1, :] - framed[:-2, 1:-1, :])
    slope_row = 0.5 * (framed[1:-1, 2:, :] - framed[1:-1, :-2, :])
    slope_col = slope_cols(center)
    inverse = lax.rsqrt(
        slope_depth * slope_depth + slope_row * slope_row + slope_col * slope_col + 1.0
    )
    lambert = jnp.abs((slope_depth + 2.0 * slope_row + 2.0 * slope_col) * inverse) / 3.0
    ambient = 0.5 * transfer[7]
    shading = ambient + (1.0 - ambient) * lambert
    depth_term = 2.0 * transfer[6] / slices * jax.nn.softplus(center)
    opacity = -jnp.expm1(-depth_term)
    tinting = jax.nn.sigmoid(2.0 * center)
    weight = shading * opacity
    emitted = jnp.stack(
        [(transfer[channel] + transfer[3 + channel] * tinting) * weight for channel in range(3)]
    )
    return (emitted, depth_term)


def blend_parts(parts):
    depth_parts = parts[:, 3]
    before = jnp.cumsum(depth_parts, 0) - depth_parts
    color = jnp.sum(jnp.exp(-before)[:, None] * parts[:, :3], 0)
    total = jnp.sum(depth_parts, 0)
    return jnp.concatenate([color, total[None]], 0)


def on_device(volume, transfer):
    local_slices, local_rows, columns = volume.shape
    groups = lax.axis_size("depth")
    slices = local_slices * groups
    padded = with_halo(volume, (("depth", 0), ("row", 1)), 1)
    steps = local_slices // 8

    def march(carry, index):
        color, depth_acc = carry
        slab = lax.dynamic_slice_in_dim(padded, index * 8, 10, 0)
        emitted, depth_term = emit(slab, transfer, slices)
        before = jnp.cumsum(depth_term, 0) - depth_term
        passing = jnp.exp(-(depth_acc[None] + before))
        color = color + jnp.sum(passing[None] * emitted, 1)
        depth_acc = depth_acc + jnp.sum(depth_term, 0)
        return ((color, depth_acc), None)

    start_color = jnp.zeros((3, local_rows, columns), jnp.float32)
    start_depth = jnp.zeros((local_rows, columns), jnp.float32)
    (color, depth_acc), unused = lax.scan(
        march, (start_color, start_depth), jnp.arange(steps, dtype=jnp.int32)
    )
    partial_image = jnp.concatenate([color, depth_acc[None]], 0)
    final = blend_parts(
        lax.all_to_all(partial_image[None], "depth", split_axis=3, concat_axis=0, tiled=True)
    )
    return jnp.concatenate([final[:3], -jnp.expm1(-final[3:4])], 0)


def solution(mesh):
    in_specs = (P("depth", "row", None), P())
    out_specs = P(None, "row", "depth")
    return jax.shard_map(
        on_device, mesh=mesh, in_specs=in_specs, out_specs=out_specs, check_vma=False
    )
```

profile of v0, /device:TPU:14, one launch (start us, length us, event | category | flops | bytes accessed | tf_op | source)
XLA Modules:
  0.0 483.0 jit_solution(13706453914436330940)
XLA Ops:
  0.0 1.3 fusion.12
  1.3 1.8 collective-permute-start
  3.1 1.3 collective-permute-start.1
  4.6 10.6 %constant_dynamic-update-slice_fusion.1 = f32[50,64,2048]{2,1,0:T(8,128)S(1)} fusion(f32[50,64,2048]{2,1,0:T(8,128)S(1)} %constant_dynamic-update-slice_fusion.2, f32[48,64,2048]{2,1,0:T(8,128)} %param.4), kind=kLoop, calls=%fused_computation.28 | loop fusion | bytes 50331648
  15.3 0.8 fusion.11
  16.1 3.4 collective-permute-start.2
  19.5 4.4 copy-done.2
  24.0 2.7 collective-permute-start.3
  26.7 0.7 fusion.13
  28.7 7.4 %collective-permute-done.3 = f32[50,1,2048]{2,1,0:T(1,128)} collective-permute-done((f32[50,1,2048]{2,1,0:T(1,128)S(1)}, f32[50,1,2048]{2,1,0:T(1,128)}, u32[]{:S(2)}, u32[]{:S(2)}) %collective-permute-start.3) | collective-permute-done | bytes 409632 | tf_op jit(solution)/shard_map/ppermute | solution.py:17
  36.0 20.7 %pad_maximum_fusion = f32[50,66,2048]{2,1,0:T(8,128)} fusion(f32[50,1,2048]{2,1,0:T(1,128)} %collective-permute-done.3, f32[50,64,2048]{2,1,0:T(8,128)} %copy-done.2, f32[50,1,2048]{2,1,0:T(1,128)S(1)} %collective-permute-done.2), kind=kLoop, calls=%fused_computation.17 | loop fusion | flops 13516800 | bytes 54067200 | tf_op jit(solution)/shard_map/concatenate | solution.py:13
  56.7 343.4 %while.16 = (s32[]{:T(128)}, f32[3,64,2048]{2,1,0:T(8,128)S(1)}, f32[64,2048]{1,0:T(8,128)S(1)}, f32[]{:T(128)}, s32[6]{0:T(128)S(1)}, /*index=5*/f32[50,66,2048...) while((s32[]{:T(128)}, f32[3,64,2048]{2,1,0:T(8,128)S(1)}, ...), condition=%wide.region_4.5_spmd.clone, body=%wide.region_0.4_spmd.clone.sunk | while | flops 86507528 | bytes 139449296 | solution.py:79
  56.7 0.6 dynamic_slice.18
  57.8 8.3 %fusion.22 = (f32[8,64,2047]{2,1,0:T(8,128)}, f32[8,64,2047]{2,1,0:T(8,128)}) fusion(f32[50,66,2048]{2,1,0:T(8,128)} %get-tuple-element.322, s32[]{:T(128)S(6)} %add.257, s32[]{:T(128)S(6)} %add.258), kind=kLoop, calls=%fused_computation.31.clone.1 | loop fusion | bytes 16769032 | tf_op jit(solution)/shard_map/while/body/eval_jaxpr/slice | solution.py:26
  66.1 0.7 fusion.21
  66.7 18.1 %multiply_bitcast_fusion.5 = (f32[1,8,64,2048]{3,2,1,0:T(8,128)}, f32[8,64,2048]{2,1,0:T(8,128)S(1)}) fusion(f32[]{:T(128)} %bitcast.41, f32[]{:T(128)} %bitcast.42, f32[50,66,2048]{2,1,0:T(8,128)} %get-tuple-element.322, s32[]{:T(128)S(6)} %add.257, s32[]{:T(128)S(6)} %add.258, f32[]{:T(128)} %get-tuple-element.320, f32[]{:T(128)} %get-tuple-element.325, ...), kind=kLoop, calls=%fused_computation.9.clone.1 | loop fusion | flops 36700160 | bytes 37744680 | tf_op jit(solution)/shard_map/while/body/eval_jaxpr/stack | solution.py:46
  84.9 10.4 %multiply_bitcast_fusion.6 = (f32[1,8,64,2048]{3,2,1,0:T(8,128)}, f32[1,8,64,2048]{3,2,1,0:T(8,128)}, f32[64,2048]{1,0:T(8,128)S(1)}) fusion(f32[8,64,2048]{2,1,0:T(8,128)S(1)} %get-tuple-element.276, f32[]{:T(128)} %bitcast.44, f32[]{:T(128)} %bitcast.45, f32[50,66,2048]{2,1,0:T(8,128)} %get-tuple-element.322, s32[]{:T(128)S(6)} %add.257, ...), kind=kLoop, calls=%fused_computation.8.clone.1 | loop fusion | flops 18743296 | bytes 17301532 | tf_op jit(solution)/shard_map/while/body/eval_jaxpr/stack | solution.py:46
  95.5 12.9 %negate_exponential_fusion.3 = f32[8,64,2048]{2,1,0:T(8,128)S(1)} fusion(f32[64,2048]{1,0:T(8,128)S(1)} %get-tuple-element.285, f32[50,66,2048]{2,1,0:T(8,128)} %get-tuple-element.322, s32[]{:T(128)S(6)} %add.257, s32[]{:T(128)S(6)} %add.258, f32[]{:T(128)} %get-tuple-element.320), kind=kOutput, calls=%fused_computation.12.clone.1 | output fusion | flops 17825792 | bytes 8913416 | tf_op jit(solution)/shard_map/while/body/eval_jaxpr/jit(cumsum)/reduce_window_sum | solution.py:71
  108.4 4.0 fusion.24
  112.4 0.5 select_add_fusion.2
  112.9 0.6 dynamic_slice.18
  114.1 8.3 %fusion.22 = (f32[8,64,2047]{2,1,0:T(8,128)}, f32[8,64,2047]{2,1,0:T(8,128)}) fusion(f32[50,66,2048]{2,1,0:T(8,128)} %get-tuple-element.322, s32[]{:T(128)S(6)} %add.257, s32[]{:T(128)S(6)} %add.258), kind=kLoop, calls=%fused_computation.31.clone.1 | loop fusion | bytes 16769032 | tf_op jit(solution)/shard_map/while/body/eval_jaxpr/slice | solution.py:26
  122.3 0.7 fusion.21
  123.0 18.2 %multiply_bitcast_fusion.5 = (f32[1,8,64,2048]{3,2,1,0:T(8,128)}, f32[8,64,2048]{2,1,0:T(8,128)S(1)}) fusion(f32[]{:T(128)} %bitcast.41, f32[]{:T(128)} %bitcast.42, f32[50,66,2048]{2,1,0:T(8,128)} %get-tuple-element.322, s32[]{:T(128)S(6)} %add.257, s32[]{:T(128)S(6)} %add.258, f32[]{:T(128)} %get-tuple-element.320, f32[]{:T(128)} %get-tuple-element.325, ...), kind=kLoop, calls=%fused_computation.9.clone.1 | loop fusion | flops 36700160 | bytes 37744680 | tf_op jit(solution)/shard_map/while/body/eval_jaxpr/stack | solution.py:46
  141.2 10.4 %multiply_bitcast_fusion.6 = (f32[1,8,64,2048]{3,2,1,0:T(8,128)}, f32[1,8,64,2048]{3,2,1,0:T(8,128)}, f32[64,2048]{1,0:T(8,128)S(1)}) fusion(f32[8,64,2048]{2,1,0:T(8,128)S(1)} %get-tuple-element.276, f32[]{:T(128)} %bitcast.44, f32[]{:T(128)} %bitcast.45, f32[50,66,2048]{2,1,0:T(8,128)} %get-tuple-element.322, s32[]{:T(128)S(6)} %add.257, ...), kind=kLoop, calls=%fused_computation.8.clone.1 | loop fusion | flops 18743296 | bytes 17301532 | tf_op jit(solution)/shard_map/while/body/eval_jaxpr/stack | solution.py:46
  151.9 14.1 %negate_exponential_fusion.3 = f32[8,64,2048]{2,1,0:T(8,128)S(1)} fusion(f32[64,2048]{1,0:T(8,128)S(1)} %get-tuple-element.285, f32[50,66,2048]{2,1,0:T(8,128)} %get-tuple-element.322, s32[]{:T(128)S(6)} %add.257, s32[]{:T(128)S(6)} %add.258, f32[]{:T(128)} %get-tuple-element.320), kind=kOutput, calls=%fused_computation.12.clone.1 | output fusion | flops 17825792 | bytes 8913416 | tf_op jit(solution)/shard_map/while/body/eval_jaxpr/jit(cumsum)/reduce_window_sum | solution.py:71
  166.0 4.0 fusion.24
  170.5 0.6 dynamic_slice.18
  171.6 8.3 %fusion.22 = (f32[8,64,2047]{2,1,0:T(8,128)}, f32[8,64,2047]{2,1,0:T(8,128)}) fusion(f32[50,66,2048]{2,1,0:T(8,128)} %get-tuple-element.322, s32[]{:T(128)S(6)} %add.257, s32[]{:T(128)S(6)} %add.258), kind=kLoop, calls=%fused_computation.31.clone.1 | loop fusion | bytes 16769032 | tf_op jit(solution)/shard_map/while/body/eval_jaxpr/slice | solution.py:26
  179.9 0.7 fusion.21
  180.6 18.1 %multiply_bitcast_fusion.5 = (f32[1,8,64,2048]{3,2,1,0:T(8,128)}, f32[8,64,2048]{2,1,0:T(8,128)S(1)}) fusion(f32[]{:T(128)} %bitcast.41, f32[]{:T(128)} %bitcast.42, f32[50,66,2048]{2,1,0:T(8,128)} %get-tuple-element.322, s32[]{:T(128)S(6)} %add.257, s32[]{:T(128)S(6)} %add.258, f32[]{:T(128)} %get-tuple-element.320, f32[]{:T(128)} %get-tuple-element.325, ...), kind=kLoop, calls=%fused_computation.9.clone.1 | loop fusion | flops 36700160 | bytes 37744680 | tf_op jit(solution)/shard_map/while/body/eval_jaxpr/stack | solution.py:46
  198.7 10.4 %multiply_bitcast_fusion.6 = (f32[1,8,64,2048]{3,2,1,0:T(8,128)}, f32[1,8,64,2048]{3,2,1,0:T(8,128)}, f32[64,2048]{1,0:T(8,128)S(1)}) fusion(f32[8,64,2048]{2,1,0:T(8,128)S(1)} %get-tuple-element.276, f32[]{:T(128)} %bitcast.44, f32[]{:T(128)} %bitcast.45, f32[50,66,2048]{2,1,0:T(8,128)} %get-tuple-element.322, s32[]{:T(128)S(6)} %add.257, ...), kind=kLoop, calls=%fused_computation.8.clone.1 | loop fusion | flops 18743296 | bytes 17301532 | tf_op jit(solution)/shard_map/while/body/eval_jaxpr/stack | solution.py:46
  209.3 14.2 %negate_exponential_fusion.3 = f32[8,64,2048]{2,1,0:T(8,128)S(1)} fusion(f32[64,2048]{1,0:T(8,128)S(1)} %get-tuple-element.285, f32[50,66,2048]{2,1,0:T(8,128)} %get-tuple-element.322, s32[]{:T(128)S(6)} %add.257, s32[]{:T(128)S(6)} %add.258, f32[]{:T(128)} %get-tuple-element.320), kind=kOutput, calls=%fused_computation.12.clone.1 | output fusion | flops 17825792 | bytes 8913416 | tf_op jit(solution)/shard_map/while/body/eval_jaxpr/jit(cumsum)/reduce_window_sum | solution.py:71
  223.5 4.0 fusion.24
  228.0 0.6 dynamic_slice.18
  229.1 8.3 %fusion.22 = (f32[8,64,2047]{2,1,0:T(8,128)}, f32[8,64,2047]{2,1,0:T(8,128)}) fusion(f32[50,66,2048]{2,1,0:T(8,128)} %get-tuple-element.322, s32[]{:T(128)S(6)} %add.257, s32[]{:T(128)S(6)} %add.258), kind=kLoop, calls=%fused_computation.31.clone.1 | loop fusion | bytes 16769032 | tf_op jit(solution)/shard_map/while/body/eval_jaxpr/slice | solution.py:26
  237.4 0.7 fusion.21
  238.1 17.9 %multiply_bitcast_fusion.5 = (f32[1,8,64,2048]{3,2,1,0:T(8,128)}, f32[8,64,2048]{2,1,0:T(8,128)S(1)}) fusion(f32[]{:T(128)} %bitcast.41, f32[]{:T(128)} %bitcast.42, f32[50,66,2048]{2,1,0:T(8,128)} %get-tuple-element.322, s32[]{:T(128)S(6)} %add.257, s32[]{:T(128)S(6)} %add.258, f32[]{:T(128)} %get-tuple-element.320, f32[]{:T(128)} %get-tuple-element.325, ...), kind=kLoop, calls=%fused_computation.9.clone.1 | loop fusion | flops 36700160 | bytes 37744680 | tf_op jit(solution)/shard_map/while/body/eval_jaxpr/stack | solution.py:46
  256.0 10.4 %multiply_bitcast_fusion.6 = (f32[1,8,64,2048]{3,2,1,0:T(8,128)}, f32[1,8,64,2048]{3,2,1,0:T(8,128)}, f32[64,2048]{1,0:T(8,128)S(1)}) fusion(f32[8,64,2048]{2,1,0:T(8,128)S(1)} %get-tuple-element.276, f32[]{:T(128)} %bitcast.44, f32[]{:T(128)} %bitcast.45, f32[50,66,2048]{2,1,0:T(8,128)} %get-tuple-element.322, s32[]{:T(128)S(6)} %add.257, ...), kind=kLoop, calls=%fused_computation.8.clone.1 | loop fusion | flops 18743296 | bytes 17301532 | tf_op jit(solution)/shard_map/while/body/eval_jaxpr/stack | solution.py:46
  266.6 13.8 %negate_exponential_fusion.3 = f32[8,64,2048]{2,1,0:T(8,128)S(1)} fusion(f32[64,2048]{1,0:T(8,128)S(1)} %get-tuple-element.285, f32[50,66,2048]{2,1,0:T(8,128)} %get-tuple-element.322, s32[]{:T(128)S(6)} %add.257, s32[]{:T(128)S(6)} %add.258, f32[]{:T(128)} %get-tuple-element.320), kind=kOutput, calls=%fused_computation.12.clone.1 | output fusion | flops 17825792 | bytes 8913416 | tf_op jit(solution)/shard_map/while/body/eval_jaxpr/jit(cumsum)/reduce_window_sum | solution.py:71
  280.4 4.0 fusion.24
  285.0 0.6 dynamic_slice.18
  286.1 8.3 %fusion.22 = (f32[8,64,2047]{2,1,0:T(8,128)}, f32[8,64,2047]{2,1,0:T(8,128)}) fusion(f32[50,66,2048]{2,1,0:T(8,128)} %get-tuple-element.322, s32[]{:T(128)S(6)} %add.257, s32[]{:T(128)S(6)} %add.258), kind=kLoop, calls=%fused_computation.31.clone.1 | loop fusion | bytes 16769032 | tf_op jit(solution)/shard_map/while/body/eval_jaxpr/slice | solution.py:26
  294.4 0.7 fusion.21
  295.0 18.2 %multiply_bitcast_fusion.5 = (f32[1,8,64,2048]{3,2,1,0:T(8,128)}, f32[8,64,2048]{2,1,0:T(8,128)S(1)}) fusion(f32[]{:T(128)} %bitcast.41, f32[]{:T(128)} %bitcast.42, f32[50,66,2048]{2,1,0:T(8,128)} %get-tuple-element.322, s32[]{:T(128)S(6)} %add.257, s32[]{:T(128)S(6)} %add.258, f32[]{:T(128)} %get-tuple-element.320, f32[]{:T(128)} %get-tuple-element.325, ...), kind=kLoop, calls=%fused_computation.9.clone.1 | loop fusion | flops 36700160 | bytes 37744680 | tf_op jit(solution)/shard_map/while/body/eval_jaxpr/stack | solution.py:46
  313.3 10.4 %multiply_bitcast_fusion.6 = (f32[1,8,64,2048]{3,2,1,0:T(8,128)}, f32[1,8,64,2048]{3,2,1,0:T(8,128)}, f32[64,2048]{1,0:T(8,128)S(1)}) fusion(f32[8,64,2048]{2,1,0:T(8,128)S(1)} %get-tuple-element.276, f32[]{:T(128)} %bitcast.44, f32[]{:T(128)} %bitcast.45, f32[50,66,2048]{2,1,0:T(8,128)} %get-tuple-element.322, s32[]{:T(128)S(6)} %add.257, ...), kind=kLoop, calls=%fused_computation.8.clone.1 | loop fusion | flops 18743296 | bytes 17301532 | tf_op jit(solution)/shard_map/while/body/eval_jaxpr/stack | solution.py:46
  323.9 14.1 %negate_exponential_fusion.3 = f32[8,64,2048]{2,1,0:T(8,128)S(1)} fusion(f32[64,2048]{1,0:T(8,128)S(1)} %get-tuple-element.285, f32[50,66,2048]{2,1,0:T(8,128)} %get-tuple-element.322, s32[]{:T(128)S(6)} %add.257, s32[]{:T(128)S(6)} %add.258, f32[]{:T(128)} %get-tuple-element.320), kind=kOutput, calls=%fused_computation.12.clone.1 | output fusion | flops 17825792 | bytes 8913416 | tf_op jit(solution)/shard_map/while/body/eval_jaxpr/jit(cumsum)/reduce_window_sum | solution.py:71
  338.0 4.0 fusion.24
  342.6 0.6 dynamic_slice.18
  343.7 8.3 %fusion.22 = (f32[8,64,2047]{2,1,0:T(8,128)}, f32[8,64,2047]{2,1,0:T(8,128)}) fusion(f32[50,66,2048]{2,1,0:T(8,128)} %get-tuple-element.322, s32[]{:T(128)S(6)} %add.257, s32[]{:T(128)S(6)} %add.258), kind=kLoop, calls=%fused_computation.31.clone.1 | loop fusion | bytes 16769032 | tf_op jit(solution)/shard_map/while/body/eval_jaxpr/slice | solution.py:26
  351.9 0.7 fusion.21
  352.6 18.4 %multiply_bitcast_fusion.5 = (f32[1,8,64,2048]{3,2,1,0:T(8,128)}, f32[8,64,2048]{2,1,0:T(8,128)S(1)}) fusion(f32[]{:T(128)} %bitcast.41, f32[]{:T(128)} %bitcast.42, f32[50,66,2048]{2,1,0:T(8,128)} %get-tuple-element.322, s32[]{:T(128)S(6)} %add.257, s32[]{:T(128)S(6)} %add.258, f32[]{:T(128)} %get-tuple-element.320, f32[]{:T(128)} %get-tuple-element.325, ...), kind=kLoop, calls=%fused_computation.9.clone.1 | loop fusion | flops 36700160 | bytes 37744680 | tf_op jit(solution)/shard_map/while/body/eval_jaxpr/stack | solution.py:46
  371.0 10.4 %multiply_bitcast_fusion.6 = (f32[1,8,64,2048]{3,2,1,0:T(8,128)}, f32[1,8,64,2048]{3,2,1,0:T(8,128)}, f32[64,2048]{1,0:T(8,128)S(1)}) fusion(f32[8,64,2048]{2,1,0:T(8,128)S(1)} %get-tuple-element.276, f32[]{:T(128)} %bitcast.44, f32[]{:T(128)} %bitcast.45, f32[50,66,2048]{2,1,0:T(8,128)} %get-tuple-element.322, s32[]{:T(128)S(6)} %add.257, ...), kind=kLoop, calls=%fused_computation.8.clone.1 | loop fusion | flops 18743296 | bytes 17301532 | tf_op jit(solution)/shard_map/while/body/eval_jaxpr/stack | solution.py:46
  381.6 13.9 %negate_exponential_fusion.3 = f32[8,64,2048]{2,1,0:T(8,128)S(1)} fusion(f32[64,2048]{1,0:T(8,128)S(1)} %get-tuple-element.285, f32[50,66,2048]{2,1,0:T(8,128)} %get-tuple-element.322, s32[]{:T(128)S(6)} %add.257, s32[]{:T(128)S(6)} %add.258, f32[]{:T(128)} %get-tuple-element.320), kind=kOutput, calls=%fused_computation.12.clone.1 | output fusion | flops 17825792 | bytes 8913416 | tf_op jit(solution)/shard_map/while/body/eval_jaxpr/jit(cumsum)/reduce_window_sum | solution.py:71
  395.5 4.0 fusion.24
  400.0 3.1 copy.6
  403.5 5.3 %fusion.14 = f32[2048,1,4,64]{3,2,1,0:T(4,128)} fusion(f32[1,64,2048]{1,0,2:T(1,128)S(1)} %bitcast.50, f32[3,64,2048]{1,0,2:T(4,128)} %copy.6), kind=kLoop, calls=%fused_computation.36 | loop fusion | flops 524288 | bytes 4194304
  408.8 6.8 %reshape.30 = f32[8,1,65536]{2,1,0:T(1,128)S(1)} reshape(f32[2048,1,4,64]{3,2,1,0:T(4,128)} %fusion.14) | data formatting | bytes 4194304
  415.6 42.5 %all_to_all.18 = f32[8,1,65536]{2,1,0:T(1,128)} all-to-all(f32[8,1,65536]{2,1,0:T(1,128)S(1)} %reshape.30), channel_id=1, replica_groups=mesh['depth'=8,'row'=16] {'depth'}, dimensions={0} | all-to-all | bytes 4194304 | tf_op jit(solution)/shard_map/all_to_all | solution.py:84
  458.6 7.2 %reduce.1 = f32[8,65536]{1,0:T(8,128)S(1)} reduce(f32[8,1,65536]{2,1,0:T(1,128)} %all_to_all.18, f32[]{:T(128)} %broadcast.78), dimensions={1}, to_apply=%all_to_all.13.reduce_sub_computation | reduce | bytes 4194308 | tf_op jit(solution)/shard_map/all_to_all | solution.py:84
  465.8 4.8 reshape.31
  470.6 7.7 %negate_exponential_fusion.1 = (f32[8,1,64,256]{2,1,3,0:T(1,128)S(1)}, f32[64,256]{0,1:T(8,128)S(1)}) fusion(f32[8,4,64,256]{2,1,3,0:T(4,128)} %bitcast.48), kind=kOutput, calls=%fused_computation.21 | output fusion | flops 1294336 | bytes 2686976 | tf_op jit(solution)/shard_map/jit(cumsum)/reduce_window_sum | solution.py:54
  478.3 3.4 fusion.5
  482.1 0.9 copy.7
  (50 shorter events, 5.2 us)
Async XLA Ops:
  1.3 3.3 collective-permute-start
  3.1 12.2 %collective-permute-start.1 = (f32[1,64,2048]{2,1,0:T(8,128)S(1)}, f32[1,64,2048]{2,1,0:T(8,128)S(1)}, u32[]{:S(2)}, u32[]{:S(2)}) collective-permute-start(f32[1,64,2048]{2,1,0:T(8,128)S(1)} %get-tuple-element.196), channel_id=1, source_target_pairs={{16,0},{32,16},{48,32},{64,48},{80,64},{96,80},{112,96},{17,1},{33... | collective-permute-start | bytes 1572872 | tf_op jit(solution)/shard_map/ppermute | solution.py:17
  4.6 22.1 %copy-start.3 = (f32[8]{0:T(128)S(1)}, f32[8]{0:T(128)}, u32[]{:S(2)}) copy-start(f32[8]{0:T(128)} %param.5) | copy-start | bytes 100
  15.3 8.6 %copy-start.2 = (f32[50,64,2048]{2,1,0:T(8,128)}, f32[50,64,2048]{2,1,0:T(8,128)S(1)}, u32[]{:S(2)}) copy-start(f32[50,64,2048]{2,1,0:T(8,128)S(1)} %constant_dynamic-update-slice_fusion) | copy-start | bytes 78643200
  16.1 12.5 %collective-permute-start.2 = (f32[50,1,2048]{2,1,0:T(1,128)S(1)}, f32[50,1,2048]{2,1,0:T(1,128)S(1)}, u32[]{:S(2)}, u32[]{:S(2)}) collective-permute-start(f32[50,1,2048]{2,1,0:T(1,128)S(1)} %get-tuple-element.194), channel_id=1, source_target_pairs={{0,1},{1,2},{2,3},{3,4},{4,5},{5,6},{6,7},{7,8},{8,9},{9,10},{10,1... | collective-permute-start | bytes 1228808 | tf_op jit(solution)/shard_map/ppermute | solution.py:15
  24.0 12.0 %collective-permute-start.3 = (f32[50,1,2048]{2,1,0:T(1,128)S(1)}, f32[50,1,2048]{2,1,0:T(1,128)}, u32[]{:S(2)}, u32[]{:S(2)}) collective-permute-start(f32[50,1,2048]{2,1,0:T(1,128)S(1)} %get-tuple-element.195), channel_id=1, source_target_pairs={{1,0},{2,1},{3,2},{4,3},{5,4},{6,5},{7,6},{8,7},{9,8},{10,9},{11,1... | collective-permute-start | bytes 1228808 | tf_op jit(solution)/shard_map/ppermute | solution.py:17
  95.5 12.9 %copy-start = (f32[1,8,64,2048]{3,2,1,0:T(8,128)S(1)}, f32[1,8,64,2048]{3,2,1,0:T(8,128)}, u32[]{:S(2)}) copy-start(f32[1,8,64,2048]{3,2,1,0:T(8,128)} %get-tuple-element.283) | copy-start | bytes 12582916 | tf_op jit(solution)/shard_map/while
  95.5 12.9 %copy-start.1 = (f32[1,8,64,2048]{3,2,1,0:T(8,128)S(1)}, f32[1,8,64,2048]{3,2,1,0:T(8,128)}, u32[]{:S(2)}) copy-start(f32[1,8,64,2048]{3,2,1,0:T(8,128)} %get-tuple-element.282) | copy-start | bytes 12582916 | tf_op jit(solution)/shard_map/while
  151.8 14.1 %copy-start = (f32[1,8,64,2048]{3,2,1,0:T(8,128)S(1)}, f32[1,8,64,2048]{3,2,1,0:T(8,128)}, u32[]{:S(2)}) copy-start(f32[1,8,64,2048]{3,2,1,0:T(8,128)} %get-tuple-element.283) | copy-start | bytes 12582916 | tf_op jit(solution)/shard_map/while
  151.8 14.1 %copy-start.1 = (f32[1,8,64,2048]{3,2,1,0:T(8,128)S(1)}, f32[1,8,64,2048]{3,2,1,0:T(8,128)}, u32[]{:S(2)}) copy-start(f32[1,8,64,2048]{3,2,1,0:T(8,128)} %get-tuple-element.282) | copy-start | bytes 12582916 | tf_op jit(solution)/shard_map/while
  209.3 14.2 %copy-start = (f32[1,8,64,2048]{3,2,1,0:T(8,128)S(1)}, f32[1,8,64,2048]{3,2,1,0:T(8,128)}, u32[]{:S(2)}) copy-start(f32[1,8,64,2048]{3,2,1,0:T(8,128)} %get-tuple-element.283) | copy-start | bytes 12582916 | tf_op jit(solution)/shard_map/while
  209.3 14.2 %copy-start.1 = (f32[1,8,64,2048]{3,2,1,0:T(8,128)S(1)}, f32[1,8,64,2048]{3,2,1,0:T(8,128)}, u32[]{:S(2)}) copy-start(f32[1,8,64,2048]{3,2,1,0:T(8,128)} %get-tuple-element.282) | copy-start | bytes 12582916 | tf_op jit(solution)/shard_map/while
  266.6 13.8 %copy-start = (f32[1,8,64,2048]{3,2,1,0:T(8,128)S(1)}, f32[1,8,64,2048]{3,2,1,0:T(8,128)}, u32[]{:S(2)}) copy-start(f32[1,8,64,2048]{3,2,1,0:T(8,128)} %get-tuple-element.283) | copy-start | bytes 12582916 | tf_op jit(solution)/shard_map/while
  266.6 13.8 %copy-start.1 = (f32[1,8,64,2048]{3,2,1,0:T(8,128)S(1)}, f32[1,8,64,2048]{3,2,1,0:T(8,128)}, u32[]{:S(2)}) copy-start(f32[1,8,64,2048]{3,2,1,0:T(8,128)} %get-tuple-element.282) | copy-start | bytes 12582916 | tf_op jit(solution)/shard_map/while
  323.9 14.2 %copy-start = (f32[1,8,64,2048]{3,2,1,0:T(8,128)S(1)}, f32[1,8,64,2048]{3,2,1,0:T(8,128)}, u32[]{:S(2)}) copy-start(f32[1,8,64,2048]{3,2,1,0:T(8,128)} %get-tuple-element.283) | copy-start | bytes 12582916 | tf_op jit(solution)/shard_map/while
  323.9 14.2 %copy-start.1 = (f32[1,8,64,2048]{3,2,1,0:T(8,128)S(1)}, f32[1,8,64,2048]{3,2,1,0:T(8,128)}, u32[]{:S(2)}) copy-start(f32[1,8,64,2048]{3,2,1,0:T(8,128)} %get-tuple-element.282) | copy-start | bytes 12582916 | tf_op jit(solution)/shard_map/while
  381.6 13.9 %copy-start = (f32[1,8,64,2048]{3,2,1,0:T(8,128)S(1)}, f32[1,8,64,2048]{3,2,1,0:T(8,128)}, u32[]{:S(2)}) copy-start(f32[1,8,64,2048]{3,2,1,0:T(8,128)} %get-tuple-element.283) | copy-start | bytes 12582916 | tf_op jit(solution)/shard_map/while
  381.6 13.9 %copy-start.1 = (f32[1,8,64,2048]{3,2,1,0:T(8,128)S(1)}, f32[1,8,64,2048]{3,2,1,0:T(8,128)}, u32[]{:S(2)}) copy-start(f32[1,8,64,2048]{3,2,1,0:T(8,128)} %get-tuple-element.282) | copy-start | bytes 12582916 | tf_op jit(solution)/shard_map/while
where the time goes:
time: 484 us; the launch traced here: 483 us
  other arithmetic  327 us (68%)
  local copies, waits for them, and re-layouts  91.4 us (19%)
  blocking collectives  42.5 us (9%)
  starting transfers between devices  9.19 us (2%)
  waiting for transfers between devices  7.54 us (2%)
    another operation x12, other arithmetic, emit(): jnp.stack([(transfer[channel] + transfer[3 + channel] * tinting) * weight...  172 us
    another operation x6, other arithmetic, march(): before = jnp.cumsum(depth_term, 0) - depth_term  83 us
    slice x6, local copies, waits for them, and re-layouts, slope_cols(): right = jnp.concatenate([center[..., 1:], zero_col], -1)  49.7 us
    all_to_all x1, blocking collectives, on_device(): lax.all_to_all(partial_image[None], 'depth', split_axis=3, concat_axis=0,...  42.5 us
    unnamed x8, local copies, waits for them, and re-layouts  26.7 us
    reduce_sum x6, other arithmetic, march(): color = color + jnp.sum(passing[None] * emitted, 1)  23.7 us
    concatenate x1, other arithmetic, with_halo(): jnp.concatenate([lax.ppermute(tail, axis, [(i, (i + 1) % count) for i in...  20.7 us
  transfers between devices with their start and end apart: 4, of which 2 were waited for; matrix products, arithmetic and copies ran while one was open for 2% of the time, Pallas kernels for 0%

commit v1 on v0

--- a/solution.py
+++ b/solution.py
@@ -2,6 +2,29 @@
 import jax.numpy as jnp
 from jax import lax
 from jax.sharding import PartitionSpec as P
+
+
+def split_up(x, dim, count):
+    lengths = x.shape
+    blocks = x.reshape(*lengths[:dim], count, lengths[dim] // count, *lengths[dim + 1 :])
+    return jnp.moveaxis(blocks, dim, 0)
+
+
+def joined_along(blocks, dim):
+    lengths = list(blocks.shape[1:])
+    lengths[dim] *= blocks.shape[0]
+    return jnp.moveaxis(blocks, 0, dim).reshape(lengths)
+
+
+def swapped_with_each(x, axis, split_dim, concat_dim):
+    size, index = (lax.axis_size(axis), lax.axis_index(axis))
+    blocks = split_up(x, split_dim, size)
+    gathered = [blocks[index]]
+    for step in range(1, size):
+        sent = blocks[index ^ step]
+        gathered.append(lax.ppermute(sent, axis, [(i, i ^ step) for i in range(size)]))
+    blocks = jnp.stack(gathered)[index ^ jnp.arange(size)]
+    return joined_along(blocks, concat_dim)
 
 
 def with_halo(cells, sides, width):
@@ -80,9 +103,7 @@
         march, (start_color, start_depth), jnp.arange(steps, dtype=jnp.int32)
     )
     partial_image = jnp.concatenate([color, depth_acc[None]], 0)
-    final = blend_parts(
-        lax.all_to_all(partial_image[None], "depth", split_axis=3, concat_axis=0, tiled=True)
-    )
+    final = blend_parts(swapped_with_each(partial_image[None], "depth", 3, 0))
     return jnp.concatenate([final[:3], -jnp.expm1(-final[3:4])], 0)
 
 

time: 484 us -> 460 us (0.950)
  blocking collectives: 42.5 us -> 0 us
  waiting for transfers between devices: 7.54 us -> 30 us
  other arithmetic: 327 us -> 307 us
  starting transfers between devices: 9.19 us -> 27.9 us
  local copies, waits for them, and re-layouts: 91.4 us -> 86.1 us
    all_to_all x1 -> x0, blocking collectives: 42.5 us -> none  [on_device(): lax.all_to_all(partial_image[None], 'depth', split_axis=3, concat_axis=0,...]
    ppermute x0 -> x7, waiting for transfers between devices: none -> 22.3 us  [swapped_with_each(): lax.ppermute(sent, axis, [(i, i ^ step) for i in range(size)])]
    ppermute x0 -> x7, starting transfers between devices: none -> 19 us  [swapped_with_each(): lax.ppermute(sent, axis, [(i, i ^ step) for i in range(size)])]
    another operation x1, other arithmetic: 7.68 us -> 0.14 us  [blend_parts(): before = jnp.cumsum(depth_parts, 0) - depth_parts]
    all_to_all x1 -> x0, other arithmetic: 7.22 us -> none  [on_device(): lax.all_to_all(partial_image[None], 'depth', split_axis=3, concat_axis=0,...]
    unnamed x3 -> x2, other arithmetic: 5.27 us -> 0.01 us
    unnamed x8 -> x18, local copies, waits for them, and re-layouts: 26.7 us -> 22.1 us
  transfers between devices with their start and end apart: 4 -> 11, of which waited for: 2 -> 8; matrix products, arithmetic and copies ran while one was open for 2% -> 3% of each run, Pallas kernels for 0% -> 0%
where the time goes in v1:
time: 460 us; the launch traced here: 458 us
  other arithmetic  307 us (67%)
  local copies, waits for them, and re-layouts  86.1 us (19%)
  waiting for transfers between devices  30 us (7%)
  starting transfers between devices  27.9 us (6%)
  loops' own time  4.87 us (1%)
    another operation x12, other arithmetic, emit(): jnp.stack([(transfer[channel] + transfer[3 + channel] * tinting) * weight...  173 us
    another operation x6, other arithmetic, march(): before = jnp.cumsum(depth_term, 0) - depth_term  84.5 us
    slice x6, local copies, waits for them, and re-layouts, slope_cols(): right = jnp.concatenate([center[..., 1:], zero_col], -1)  49.8 us
    reduce_sum x6, other arithmetic, march(): color = color + jnp.sum(passing[None] * emitted, 1)  23.7 us
    ppermute x7, waiting for transfers between devices, swapped_with_each(): lax.ppermute(sent, axis, [(i, i ^ step) for i in range(size)])  22.3 us
    unnamed x18, local copies, waits for them, and re-layouts  22.1 us
    concatenate x1, other arithmetic, with_halo(): jnp.concatenate([lax.ppermute(tail, axis, [(i, (i + 1) % count) for i in...  20.7 us
    ppermute x7, starting transfers between devices, swapped_with_each(): lax.ppermute(sent, axis, [(i, i ^ step) for i in range(size)])  19 us
  transfers between devices with their start and end apart: 11, of which 8 were waited for; matrix products, arithmetic and copies ran while one was open for 3% of the time, Pallas kernels for 0%

profile of v1, /device:TPU:14, one launch (start us, length us, event | category | flops | bytes accessed | tf_op | source)
XLA Modules:
  0.0 457.9 jit_solution(15560646196273231076)
XLA Ops:
  0.0 1.3 fusion.15
  1.3 1.8 collective-permute-start
  3.1 1.3 collective-permute-start.1
  4.6 10.6 %constant_dynamic-update-slice_fusion.1 = f32[50,64,2048]{2,1,0:T(8,128)S(1)} fusion(f32[50,64,2048]{2,1,0:T(8,128)S(1)} %constant_dynamic-update-slice_fusion.2, f32[48,64,2048]{2,1,0:T(8,128)} %param.4), kind=kLoop, calls=%fused_computation.47 | loop fusion | bytes 50331648
  15.3 8.6 %copy-done.2 = f32[50,64,2048]{2,1,0:T(8,128)} copy-done((f32[50,64,2048]{2,1,0:T(8,128)}, f32[50,64,2048]{2,1,0:T(8,128)S(1)}, u32[]{:S(2)}) %copy-start.2) | copy-done | bytes 26214424
  24.0 0.8 fusion.14
  24.7 3.4 collective-permute-start.2
  28.1 2.4 collective-permute-start.3
  32.7 1.9 collective-permute-done.2
  34.6 5.6 %collective-permute-done.3 = f32[50,1,2048]{2,1,0:T(1,128)} collective-permute-done((f32[50,1,2048]{2,1,0:T(1,128)S(1)}, f32[50,1,2048]{2,1,0:T(1,128)}, u32[]{:S(2)}, u32[]{:S(2)}) %collective-permute-start.3) | collective-permute-done | bytes 409632 | tf_op jit(solution)/shard_map/ppermute | solution.py:40
  40.2 20.7 %pad_maximum_fusion = f32[50,66,2048]{2,1,0:T(8,128)} fusion(f32[50,1,2048]{2,1,0:T(1,128)} %collective-permute-done.3, f32[50,64,2048]{2,1,0:T(8,128)} %copy-done.2, f32[50,1,2048]{2,1,0:T(1,128)S(1)} %collective-permute-done.2), kind=kLoop, calls=%fused_computation.18 | loop fusion | flops 13516800 | bytes 54067200 | tf_op jit(solution)/shard_map/concatenate | solution.py:36
  60.9 348.4 %while.16 = (s32[]{:T(128)}, f32[3,64,2048]{2,1,0:T(8,128)S(1)}, f32[64,2048]{1,0:T(8,128)S(1)}, f32[]{:T(128)}, s32[6]{0:T(128)S(1)}, /*index=5*/f32[50,66,2048...) while((s32[]{:T(128)}, f32[3,64,2048]{2,1,0:T(8,128)S(1)}, ...), condition=%wide.region_4.5_spmd.clone, body=%wide.region_0.4_spmd.clone.sunk | while | flops 86507528 | bytes 139449296 | solution.py:102
  62.2 8.3 %fusion.24 = (f32[8,64,2047]{2,1,0:T(8,128)}, f32[8,64,2047]{2,1,0:T(8,128)}) fusion(f32[50,66,2048]{2,1,0:T(8,128)} %get-tuple-element.327, s32[]{:T(128)S(6)} %add.302, s32[]{:T(128)S(6)} %add.303), kind=kLoop, calls=%fused_computation.53.clone.1 | loop fusion | bytes 16769032 | tf_op jit(solution)/shard_map/while/body/eval_jaxpr/slice | solution.py:49
  70.5 0.7 fusion.23
  71.2 18.1 %multiply_bitcast_fusion.5 = (f32[1,8,64,2048]{3,2,1,0:T(8,128)}, f32[8,64,2048]{2,1,0:T(8,128)S(1)}) fusion(f32[]{:T(128)} %bitcast.70, f32[]{:T(128)} %bitcast.71, f32[50,66,2048]{2,1,0:T(8,128)} %get-tuple-element.327, s32[]{:T(128)S(6)} %add.302, s32[]{:T(128)S(6)} %add.303, f32[]{:T(128)} %get-tuple-element.325, f32[]{:T(128)} %get-tuple-element.330, ...), kind=kLoop, calls=%fused_computation.10.clone.1 | loop fusion | flops 36700160 | bytes 37744680 | tf_op jit(solution)/shard_map/while/body/eval_jaxpr/stack | solution.py:69
  89.3 10.6 %multiply_bitcast_fusion.6 = (f32[1,8,64,2048]{3,2,1,0:T(8,128)}, f32[1,8,64,2048]{3,2,1,0:T(8,128)}, f32[64,2048]{1,0:T(8,128)S(1)}) fusion(f32[8,64,2048]{2,1,0:T(8,128)S(1)} %get-tuple-element.281, f32[]{:T(128)} %bitcast.73, f32[]{:T(128)} %bitcast.74, f32[50,66,2048]{2,1,0:T(8,128)} %get-tuple-element.327, s32[]{:T(128)S(6)} %add.302, ...), kind=kLoop, calls=%fused_computation.9.clone.1 | loop fusion | flops 18743296 | bytes 17301532 | tf_op jit(solution)/shard_map/while/body/eval_jaxpr/stack | solution.py:69
  100.1 13.2 %negate_exponential_fusion.2 = f32[8,64,2048]{2,1,0:T(8,128)S(1)} fusion(f32[64,2048]{1,0:T(8,128)S(1)} %get-tuple-element.290, f32[50,66,2048]{2,1,0:T(8,128)} %get-tuple-element.327, s32[]{:T(128)S(6)} %add.302, s32[]{:T(128)S(6)} %add.303, f32[]{:T(128)} %get-tuple-element.325), kind=kOutput, calls=%fused_computation.13.clone.1 | output fusion | flops 17825792 | bytes 8913416 | tf_op jit(solution)/shard_map/while/body/eval_jaxpr/jit(cumsum)/reduce_window_sum | solution.py:94
  113.4 4.0 fusion.26
  117.9 0.7 dynamic_slice.29
  119.3 8.3 %fusion.24 = (f32[8,64,2047]{2,1,0:T(8,128)}, f32[8,64,2047]{2,1,0:T(8,128)}) fusion(f32[50,66,2048]{2,1,0:T(8,128)} %get-tuple-element.327, s32[]{:T(128)S(6)} %add.302, s32[]{:T(128)S(6)} %add.303), kind=kLoop, calls=%fused_computation.53.clone.1 | loop fusion | bytes 16769032 | tf_op jit(solution)/shard_map/while/body/eval_jaxpr/slice | solution.py:49
  127.6 0.7 fusion.23
  128.3 18.4 %multiply_bitcast_fusion.5 = (f32[1,8,64,2048]{3,2,1,0:T(8,128)}, f32[8,64,2048]{2,1,0:T(8,128)S(1)}) fusion(f32[]{:T(128)} %bitcast.70, f32[]{:T(128)} %bitcast.71, f32[50,66,2048]{2,1,0:T(8,128)} %get-tuple-element.327, s32[]{:T(128)S(6)} %add.302, s32[]{:T(128)S(6)} %add.303, f32[]{:T(128)} %get-tuple-element.325, f32[]{:T(128)} %get-tuple-element.330, ...), kind=kLoop, calls=%fused_computation.10.clone.1 | loop fusion | flops 36700160 | bytes 37744680 | tf_op jit(solution)/shard_map/while/body/eval_jaxpr/stack | solution.py:69
  146.6 10.6 %multiply_bitcast_fusion.6 = (f32[1,8,64,2048]{3,2,1,0:T(8,128)}, f32[1,8,64,2048]{3,2,1,0:T(8,128)}, f32[64,2048]{1,0:T(8,128)S(1)}) fusion(f32[8,64,2048]{2,1,0:T(8,128)S(1)} %get-tuple-element.281, f32[]{:T(128)} %bitcast.73, f32[]{:T(128)} %bitcast.74, f32[50,66,2048]{2,1,0:T(8,128)} %get-tuple-element.327, s32[]{:T(128)S(6)} %add.302, ...), kind=kLoop, calls=%fused_computation.9.clone.1 | loop fusion | flops 18743296 | bytes 17301532 | tf_op jit(solution)/shard_map/while/body/eval_jaxpr/stack | solution.py:69
  157.4 14.3 %negate_exponential_fusion.2 = f32[8,64,2048]{2,1,0:T(8,128)S(1)} fusion(f32[64,2048]{1,0:T(8,128)S(1)} %get-tuple-element.290, f32[50,66,2048]{2,1,0:T(8,128)} %get-tuple-element.327, s32[]{:T(128)S(6)} %add.302, s32[]{:T(128)S(6)} %add.303, f32[]{:T(128)} %get-tuple-element.325), kind=kOutput, calls=%fused_computation.13.clone.1 | output fusion | flops 17825792 | bytes 8913416 | tf_op jit(solution)/shard_map/while/body/eval_jaxpr/jit(cumsum)/reduce_window_sum | solution.py:94
  171.8 4.0 fusion.26
  177.7 8.3 %fusion.24 = (f32[8,64,2047]{2,1,0:T(8,128)}, f32[8,64,2047]{2,1,0:T(8,128)}) fusion(f32[50,66,2048]{2,1,0:T(8,128)} %get-tuple-element.327, s32[]{:T(128)S(6)} %add.302, s32[]{:T(128)S(6)} %add.303), kind=kLoop, calls=%fused_computation.53.clone.1 | loop fusion | bytes 16769032 | tf_op jit(solution)/shard_map/while/body/eval_jaxpr/slice | solution.py:49
  186.0 0.7 fusion.23
  186.7 18.2 %multiply_bitcast_fusion.5 = (f32[1,8,64,2048]{3,2,1,0:T(8,128)}, f32[8,64,2048]{2,1,0:T(8,128)S(1)}) fusion(f32[]{:T(128)} %bitcast.70, f32[]{:T(128)} %bitcast.71, f32[50,66,2048]{2,1,0:T(8,128)} %get-tuple-element.327, s32[]{:T(128)S(6)} %add.302, s32[]{:T(128)S(6)} %add.303, f32[]{:T(128)} %get-tuple-element.325, f32[]{:T(128)} %get-tuple-element.330, ...), kind=kLoop, calls=%fused_computation.10.clone.1 | loop fusion | flops 36700160 | bytes 37744680 | tf_op jit(solution)/shard_map/while/body/eval_jaxpr/stack | solution.py:69
  204.9 10.6 %multiply_bitcast_fusion.6 = (f32[1,8,64,2048]{3,2,1,0:T(8,128)}, f32[1,8,64,2048]{3,2,1,0:T(8,128)}, f32[64,2048]{1,0:T(8,128)S(1)}) fusion(f32[8,64,2048]{2,1,0:T(8,128)S(1)} %get-tuple-element.281, f32[]{:T(128)} %bitcast.73, f32[]{:T(128)} %bitcast.74, f32[50,66,2048]{2,1,0:T(8,128)} %get-tuple-element.327, s32[]{:T(128)S(6)} %add.302, ...), kind=kLoop, calls=%fused_computation.9.clone.1 | loop fusion | flops 18743296 | bytes 17301532 | tf_op jit(solution)/shard_map/while/body/eval_jaxpr/stack | solution.py:69
  215.7 14.2 %negate_exponential_fusion.2 = f32[8,64,2048]{2,1,0:T(8,128)S(1)} fusion(f32[64,2048]{1,0:T(8,128)S(1)} %get-tuple-element.290, f32[50,66,2048]{2,1,0:T(8,128)} %get-tuple-element.327, s32[]{:T(128)S(6)} %add.302, s32[]{:T(128)S(6)} %add.303, f32[]{:T(128)} %get-tuple-element.325), kind=kOutput, calls=%fused_computation.13.clone.1 | output fusion | flops 17825792 | bytes 8913416 | tf_op jit(solution)/shard_map/while/body/eval_jaxpr/jit(cumsum)/reduce_window_sum | solution.py:94
  229.9 4.0 fusion.26
  235.8 8.3 %fusion.24 = (f32[8,64,2047]{2,1,0:T(8,128)}, f32[8,64,2047]{2,1,0:T(8,128)}) fusion(f32[50,66,2048]{2,1,0:T(8,128)} %get-tuple-element.327, s32[]{:T(128)S(6)} %add.302, s32[]{:T(128)S(6)} %add.303), kind=kLoop, calls=%fused_computation.53.clone.1 | loop fusion | bytes 16769032 | tf_op jit(solution)/shard_map/while/body/eval_jaxpr/slice | solution.py:49
  244.1 0.7 fusion.23
  244.8 18.1 %multiply_bitcast_fusion.5 = (f32[1,8,64,2048]{3,2,1,0:T(8,128)}, f32[8,64,2048]{2,1,0:T(8,128)S(1)}) fusion(f32[]{:T(128)} %bitcast.70, f32[]{:T(128)} %bitcast.71, f32[50,66,2048]{2,1,0:T(8,128)} %get-tuple-element.327, s32[]{:T(128)S(6)} %add.302, s32[]{:T(128)S(6)} %add.303, f32[]{:T(128)} %get-tuple-element.325, f32[]{:T(128)} %get-tuple-element.330, ...), kind=kLoop, calls=%fused_computation.10.clone.1 | loop fusion | flops 36700160 | bytes 37744680 | tf_op jit(solution)/shard_map/while/body/eval_jaxpr/stack | solution.py:69
  262.8 10.6 %multiply_bitcast_fusion.6 = (f32[1,8,64,2048]{3,2,1,0:T(8,128)}, f32[1,8,64,2048]{3,2,1,0:T(8,128)}, f32[64,2048]{1,0:T(8,128)S(1)}) fusion(f32[8,64,2048]{2,1,0:T(8,128)S(1)} %get-tuple-element.281, f32[]{:T(128)} %bitcast.73, f32[]{:T(128)} %bitcast.74, f32[50,66,2048]{2,1,0:T(8,128)} %get-tuple-element.327, s32[]{:T(128)S(6)} %add.302, ...), kind=kLoop, calls=%fused_computation.9.clone.1 | loop fusion | flops 18743296 | bytes 17301532 | tf_op jit(solution)/shard_map/while/body/eval_jaxpr/stack | solution.py:69
  273.6 14.2 %negate_exponential_fusion.2 = f32[8,64,2048]{2,1,0:T(8,128)S(1)} fusion(f32[64,2048]{1,0:T(8,128)S(1)} %get-tuple-element.290, f32[50,66,2048]{2,1,0:T(8,128)} %get-tuple-element.327, s32[]{:T(128)S(6)} %add.302, s32[]{:T(128)S(6)} %add.303, f32[]{:T(128)} %get-tuple-element.325), kind=kOutput, calls=%fused_computation.13.clone.1 | output fusion | flops 17825792 | bytes 8913416 | tf_op jit(solution)/shard_map/while/body/eval_jaxpr/jit(cumsum)/reduce_window_sum | solution.py:94
  287.9 4.0 fusion.26
  292.4 0.7 dynamic_slice.29
  293.8 8.3 %fusion.24 = (f32[8,64,2047]{2,1,0:T(8,128)}, f32[8,64,2047]{2,1,0:T(8,128)}) fusion(f32[50,66,2048]{2,1,0:T(8,128)} %get-tuple-element.327, s32[]{:T(128)S(6)} %add.302, s32[]{:T(128)S(6)} %add.303), kind=kLoop, calls=%fused_computation.53.clone.1 | loop fusion | bytes 16769032 | tf_op jit(solution)/shard_map/while/body/eval_jaxpr/slice | solution.py:49
  302.1 0.7 fusion.23
  302.8 18.6 %multiply_bitcast_fusion.5 = (f32[1,8,64,2048]{3,2,1,0:T(8,128)}, f32[8,64,2048]{2,1,0:T(8,128)S(1)}) fusion(f32[]{:T(128)} %bitcast.70, f32[]{:T(128)} %bitcast.71, f32[50,66,2048]{2,1,0:T(8,128)} %get-tuple-element.327, s32[]{:T(128)S(6)} %add.302, s32[]{:T(128)S(6)} %add.303, f32[]{:T(128)} %get-tuple-element.325, f32[]{:T(128)} %get-tuple-element.330, ...), kind=kLoop, calls=%fused_computation.10.clone.1 | loop fusion | flops 36700160 | bytes 37744680 | tf_op jit(solution)/shard_map/while/body/eval_jaxpr/stack | solution.py:69
  321.3 10.6 %multiply_bitcast_fusion.6 = (f32[1,8,64,2048]{3,2,1,0:T(8,128)}, f32[1,8,64,2048]{3,2,1,0:T(8,128)}, f32[64,2048]{1,0:T(8,128)S(1)}) fusion(f32[8,64,2048]{2,1,0:T(8,128)S(1)} %get-tuple-element.281, f32[]{:T(128)} %bitcast.73, f32[]{:T(128)} %bitcast.74, f32[50,66,2048]{2,1,0:T(8,128)} %get-tuple-element.327, s32[]{:T(128)S(6)} %add.302, ...), kind=kLoop, calls=%fused_computation.9.clone.1 | loop fusion | flops 18743296 | bytes 17301532 | tf_op jit(solution)/shard_map/while/body/eval_jaxpr/stack | solution.py:69
  332.1 14.2 %negate_exponential_fusion.2 = f32[8,64,2048]{2,1,0:T(8,128)S(1)} fusion(f32[64,2048]{1,0:T(8,128)S(1)} %get-tuple-element.290, f32[50,66,2048]{2,1,0:T(8,128)} %get-tuple-element.327, s32[]{:T(128)S(6)} %add.302, s32[]{:T(128)S(6)} %add.303, f32[]{:T(128)} %get-tuple-element.325), kind=kOutput, calls=%fused_computation.13.clone.1 | output fusion | flops 17825792 | bytes 8913416 | tf_op jit(solution)/shard_map/while/body/eval_jaxpr/jit(cumsum)/reduce_window_sum | solution.py:94
  346.3 4.0 fusion.26
  352.2 8.3 %fusion.24 = (f32[8,64,2047]{2,1,0:T(8,128)}, f32[8,64,2047]{2,1,0:T(8,128)}) fusion(f32[50,66,2048]{2,1,0:T(8,128)} %get-tuple-element.327, s32[]{:T(128)S(6)} %add.302, s32[]{:T(128)S(6)} %add.303), kind=kLoop, calls=%fused_computation.53.clone.1 | loop fusion | bytes 16769032 | tf_op jit(solution)/shard_map/while/body/eval_jaxpr/slice | solution.py:49
  360.5 0.7 fusion.23
  361.2 18.3 %multiply_bitcast_fusion.5 = (f32[1,8,64,2048]{3,2,1,0:T(8,128)}, f32[8,64,2048]{2,1,0:T(8,128)S(1)}) fusion(f32[]{:T(128)} %bitcast.70, f32[]{:T(128)} %bitcast.71, f32[50,66,2048]{2,1,0:T(8,128)} %get-tuple-element.327, s32[]{:T(128)S(6)} %add.302, s32[]{:T(128)S(6)} %add.303, f32[]{:T(128)} %get-tuple-element.325, f32[]{:T(128)} %get-tuple-element.330, ...), kind=kLoop, calls=%fused_computation.10.clone.1 | loop fusion | flops 36700160 | bytes 37744680 | tf_op jit(solution)/shard_map/while/body/eval_jaxpr/stack | solution.py:69
  379.5 10.6 %multiply_bitcast_fusion.6 = (f32[1,8,64,2048]{3,2,1,0:T(8,128)}, f32[1,8,64,2048]{3,2,1,0:T(8,128)}, f32[64,2048]{1,0:T(8,128)S(1)}) fusion(f32[8,64,2048]{2,1,0:T(8,128)S(1)} %get-tuple-element.281, f32[]{:T(128)} %bitcast.73, f32[]{:T(128)} %bitcast.74, f32[50,66,2048]{2,1,0:T(8,128)} %get-tuple-element.327, s32[]{:T(128)S(6)} %add.302, ...), kind=kLoop, calls=%fused_computation.9.clone.1 | loop fusion | flops 18743296 | bytes 17301532 | tf_op jit(solution)/shard_map/while/body/eval_jaxpr/stack | solution.py:69
  390.3 14.2 %negate_exponential_fusion.2 = f32[8,64,2048]{2,1,0:T(8,128)S(1)} fusion(f32[64,2048]{1,0:T(8,128)S(1)} %get-tuple-element.290, f32[50,66,2048]{2,1,0:T(8,128)} %get-tuple-element.327, s32[]{:T(128)S(6)} %add.302, s32[]{:T(128)S(6)} %add.303, f32[]{:T(128)} %get-tuple-element.325), kind=kOutput, calls=%fused_computation.13.clone.1 | output fusion | flops 17825792 | bytes 8913416 | tf_op jit(solution)/shard_map/while/body/eval_jaxpr/jit(cumsum)/reduce_window_sum | solution.py:94
  404.6 4.0 fusion.26
  410.8 1.0 dynamic-slice_bitcast_fusion
  411.7 5.4 %collective-permute-start.4 = (f32[1,4,64,256]{3,2,1,0:T(8,128)}, f32[1,4,64,256]{3,2,1,0:T(8,128)S(1)}, u32[]{:S(2)}, u32[]{:S(2)}) collective-permute-start(f32[1,4,64,256]{3,2,1,0:T(8,128)} %get-tuple-element.204), channel_id=1, source_target_pairs={{0,16},{16,0},{32,48},{48,32},{64,80},{80,64},{96,112},{112,96},{1... | collective-permute-start | bytes 786440 | tf_op jit(solution)/shard_map/ppermute | solution.py:25
  417.1 6.6 %collective-permute-start.5 = (f32[1,4,64,256]{3,2,1,0:T(8,128)}, f32[1,4,64,256]{3,2,1,0:T(8,128)S(1)}, u32[]{:S(2)}, u32[]{:S(2)}) collective-permute-start(f32[1,4,64,256]{3,2,1,0:T(8,128)} %get-tuple-element.203), channel_id=1, source_target_pairs={{0,32},{16,48},{32,0},{48,16},{64,96},{80,112},{96,64},{112,80},{1... | collective-permute-start | bytes 786440 | tf_op jit(solution)/shard_map/ppermute | solution.py:25
  423.9 3.4 collective-permute-start.7
  427.3 1.9 collective-permute-start.9
  429.2 1.8 collective-permute-done.5
  431.1 1.6 collective-permute-start.10
  432.7 3.6 collective-permute-done.6
  436.3 7.7 %collective-permute-done.7 = f32[1,4,64,256]{3,2,1,0:T(8,128)S(1)} collective-permute-done((f32[1,4,64,256]{3,2,1,0:T(8,128)S(1)}, f32[1,4,64,256]{3,2,1,0:T(8,128)S(1)}, u32[]{:S(2)}, u32[]{:S(2)}) %collective-permute-start.7) | collective-permute-done | bytes 262176 | tf_op jit(solution)/shard_map/ppermute | solution.py:25
  444.1 5.2 %collective-permute-done.8 = f32[1,4,64,256]{3,2,1,0:T(8,128)S(1)} collective-permute-done((f32[1,4,64,256]{3,2,1,0:T(8,128)S(1)}, f32[1,4,64,256]{3,2,1,0:T(8,128)S(1)}, u32[]{:S(2)}, u32[]{:S(2)}) %collective-permute-start.8) | collective-permute-done | bytes 262176 | tf_op jit(solution)/shard_map/ppermute | solution.py:25
  449.4 3.8 collective-permute-done.10
  453.2 1.3 copy-done.3
  454.5 2.3 gather_fusion
  457.2 0.7 pad_maximum_fusion.1
  (74 shorter events, 10.0 us)
Async XLA Ops:
  1.3 3.3 collective-permute-start
  3.1 12.2 %collective-permute-start.1 = (f32[1,64,2048]{2,1,0:T(8,128)S(1)}, f32[1,64,2048]{2,1,0:T(8,128)S(1)}, u32[]{:S(2)}, u32[]{:S(2)}) collective-permute-start(f32[1,64,2048]{2,1,0:T(8,128)S(1)} %get-tuple-element.196), channel_id=1, source_target_pairs={{16,0},{32,16},{48,32},{64,48},{80,64},{96,80},{112,96},{17,1},{33... | collective-permute-start | bytes 1572872 | tf_op jit(solution)/shard_map/ppermute | solution.py:40
  4.6 26.1 %copy-start.4 = (f32[8]{0:T(128)S(1)}, f32[8]{0:T(128)}, u32[]{:S(2)}) copy-start(f32[8]{0:T(128)} %param.5) | copy-start | bytes 100
  15.3 8.6 %copy-start.2 = (f32[50,64,2048]{2,1,0:T(8,128)}, f32[50,64,2048]{2,1,0:T(8,128)S(1)}, u32[]{:S(2)}) copy-start(f32[50,64,2048]{2,1,0:T(8,128)S(1)} %constant_dynamic-update-slice_fusion) | copy-start | bytes 78643200
  24.7 9.8 %collective-permute-start.2 = (f32[50,1,2048]{2,1,0:T(1,128)S(1)}, f32[50,1,2048]{2,1,0:T(1,128)S(1)}, u32[]{:S(2)}, u32[]{:S(2)}) collective-permute-start(f32[50,1,2048]{2,1,0:T(1,128)S(1)} %get-tuple-element.194), channel_id=1, source_target_pairs={{0,1},{1,2},{2,3},{3,4},{4,5},{5,6},{6,7},{7,8},{8,9},{9,10},{10,1... | collective-permute-start | bytes 1228808 | tf_op jit(solution)/shard_map/ppermute | solution.py:38
  28.1 12.1 %collective-permute-start.3 = (f32[50,1,2048]{2,1,0:T(1,128)S(1)}, f32[50,1,2048]{2,1,0:T(1,128)}, u32[]{:S(2)}, u32[]{:S(2)}) collective-permute-start(f32[50,1,2048]{2,1,0:T(1,128)S(1)} %get-tuple-element.195), channel_id=1, source_target_pairs={{1,0},{2,1},{3,2},{4,3},{5,4},{6,5},{7,6},{8,7},{9,8},{10,9},{11,1... | collective-permute-start | bytes 1228808 | tf_op jit(solution)/shard_map/ppermute | solution.py:40
  100.1 13.3 %copy-start = (f32[1,8,64,2048]{3,2,1,0:T(8,128)S(1)}, f32[1,8,64,2048]{3,2,1,0:T(8,128)}, u32[]{:S(2)}) copy-start(f32[1,8,64,2048]{3,2,1,0:T(8,128)} %get-tuple-element.288) | copy-start | bytes 12582916 | tf_op jit(solution)/shard_map/while
  100.1 13.3 %copy-start.1 = (f32[1,8,64,2048]{3,2,1,0:T(8,128)S(1)}, f32[1,8,64,2048]{3,2,1,0:T(8,128)}, u32[]{:S(2)}) copy-start(f32[1,8,64,2048]{3,2,1,0:T(8,128)} %get-tuple-element.287) | copy-start | bytes 12582916 | tf_op jit(solution)/shard_map/while
  157.4 14.4 %copy-start = (f32[1,8,64,2048]{3,2,1,0:T(8,128)S(1)}, f32[1,8,64,2048]{3,2,1,0:T(8,128)}, u32[]{:S(2)}) copy-start(f32[1,8,64,2048]{3,2,1,0:T(8,128)} %get-tuple-element.288) | copy-start | bytes 12582916 | tf_op jit(solution)/shard_map/while
  157.4 14.4 %copy-start.1 = (f32[1,8,64,2048]{3,2,1,0:T(8,128)S(1)}, f32[1,8,64,2048]{3,2,1,0:T(8,128)}, u32[]{:S(2)}) copy-start(f32[1,8,64,2048]{3,2,1,0:T(8,128)} %get-tuple-element.287) | copy-start | bytes 12582916 | tf_op jit(solution)/shard_map/while
  215.6 14.2 %copy-start = (f32[1,8,64,2048]{3,2,1,0:T(8,128)S(1)}, f32[1,8,64,2048]{3,2,1,0:T(8,128)}, u32[]{:S(2)}) copy-start(f32[1,8,64,2048]{3,2,1,0:T(8,128)} %get-tuple-element.288) | copy-start | bytes 12582916 | tf_op jit(solution)/shard_map/while
  215.7 14.2 %copy-start.1 = (f32[1,8,64,2048]{3,2,1,0:T(8,128)S(1)}, f32[1,8,64,2048]{3,2,1,0:T(8,128)}, u32[]{:S(2)}) copy-start(f32[1,8,64,2048]{3,2,1,0:T(8,128)} %get-tuple-element.287) | copy-start | bytes 12582916 | tf_op jit(solution)/shard_map/while
  273.6 14.3 %copy-start = (f32[1,8,64,2048]{3,2,1,0:T(8,128)S(1)}, f32[1,8,64,2048]{3,2,1,0:T(8,128)}, u32[]{:S(2)}) copy-start(f32[1,8,64,2048]{3,2,1,0:T(8,128)} %get-tuple-element.288) | copy-start | bytes 12582916 | tf_op jit(solution)/shard_map/while
  273.6 14.3 %copy-start.1 = (f32[1,8,64,2048]{3,2,1,0:T(8,128)S(1)}, f32[1,8,64,2048]{3,2,1,0:T(8,128)}, u32[]{:S(2)}) copy-start(f32[1,8,64,2048]{3,2,1,0:T(8,128)} %get-tuple-element.287) | copy-start | bytes 12582916 | tf_op jit(solution)/shard_map/while
  332.1 14.2 %copy-start = (f32[1,8,64,2048]{3,2,1,0:T(8,128)S(1)}, f32[1,8,64,2048]{3,2,1,0:T(8,128)}, u32[]{:S(2)}) copy-start(f32[1,8,64,2048]{3,2,1,0:T(8,128)} %get-tuple-element.288) | copy-start | bytes 12582916 | tf_op jit(solution)/shard_map/while
  332.1 14.2 %copy-start.1 = (f32[1,8,64,2048]{3,2,1,0:T(8,128)S(1)}, f32[1,8,64,2048]{3,2,1,0:T(8,128)}, u32[]{:S(2)}) copy-start(f32[1,8,64,2048]{3,2,1,0:T(8,128)} %get-tuple-element.287) | copy-start | bytes 12582916 | tf_op jit(solution)/shard_map/while
  390.3 14.3 %copy-start = (f32[1,8,64,2048]{3,2,1,0:T(8,128)S(1)}, f32[1,8,64,2048]{3,2,1,0:T(8,128)}, u32[]{:S(2)}) copy-start(f32[1,8,64,2048]{3,2,1,0:T(8,128)} %get-tuple-element.288) | copy-start | bytes 12582916 | tf_op jit(solution)/shard_map/while
  390.3 14.3 %copy-start.1 = (f32[1,8,64,2048]{3,2,1,0:T(8,128)S(1)}, f32[1,8,64,2048]{3,2,1,0:T(8,128)}, u32[]{:S(2)}) copy-start(f32[1,8,64,2048]{3,2,1,0:T(8,128)} %get-tuple-element.287) | copy-start | bytes 12582916 | tf_op jit(solution)/shard_map/while
  411.7 15.6 %collective-permute-start.4 = (f32[1,4,64,256]{3,2,1,0:T(8,128)}, f32[1,4,64,256]{3,2,1,0:T(8,128)S(1)}, u32[]{:S(2)}, u32[]{:S(2)}) collective-permute-start(f32[1,4,64,256]{3,2,1,0:T(8,128)} %get-tuple-element.204), channel_id=1, source_target_pairs={{0,16},{16,0},{32,48},{48,32},{64,80},{80,64},{96,112},{112,96},{1... | collective-permute-start | bytes 786440 | tf_op jit(solution)/shard_map/ppermute | solution.py:25
  417.1 13.9 %collective-permute-start.5 = (f32[1,4,64,256]{3,2,1,0:T(8,128)}, f32[1,4,64,256]{3,2,1,0:T(8,128)S(1)}, u32[]{:S(2)}, u32[]{:S(2)}) collective-permute-start(f32[1,4,64,256]{3,2,1,0:T(8,128)} %get-tuple-element.203), channel_id=1, source_target_pairs={{0,32},{16,48},{32,0},{48,16},{64,96},{80,112},{96,64},{112,80},{1... | collective-permute-start | bytes 786440 | tf_op jit(solution)/shard_map/ppermute | solution.py:25
  423.7 12.6 %collective-permute-start.6 = (f32[1,4,64,256]{3,2,1,0:T(8,128)}, f32[1,4,64,256]{3,2,1,0:T(8,128)S(1)}, u32[]{:S(2)}, u32[]{:S(2)}) collective-permute-start(f32[1,4,64,256]{3,2,1,0:T(8,128)} %get-tuple-element.202), channel_id=1, source_target_pairs={{0,48},{16,32},{32,16},{48,0},{64,112},{80,96},{96,80},{112,64},{1... | collective-permute-start | bytes 786440 | tf_op jit(solution)/shard_map/ppermute | solution.py:25
  423.9 20.1 %collective-permute-start.7 = (f32[1,4,64,256]{3,2,1,0:T(8,128)S(1)}, f32[1,4,64,256]{3,2,1,0:T(8,128)S(1)}, u32[]{:S(2)}, u32[]{:S(2)}) collective-permute-start(f32[1,4,64,256]{3,2,1,0:T(8,128)S(1)} %get-tuple-element.201), channel_id=1, source_target_pairs={{0,64},{16,80},{32,96},{48,112},{64,0},{80,16},{96,32},{112,48},{1... | collective-permute-start | bytes 786440 | tf_op jit(solution)/shard_map/ppermute | solution.py:25
  427.3 22.0 %collective-permute-start.8 = (f32[1,4,64,256]{3,2,1,0:T(8,128)S(1)}, f32[1,4,64,256]{3,2,1,0:T(8,128)S(1)}, u32[]{:S(2)}, u32[]{:S(2)}) collective-permute-start(f32[1,4,64,256]{3,2,1,0:T(8,128)S(1)} %get-tuple-element.200), channel_id=1, source_target_pairs={{0,80},{16,64},{32,112},{48,96},{64,16},{80,0},{96,48},{112,32},{1... | collective-permute-start | bytes 786440 | tf_op jit(solution)/shard_map/ppermute | solution.py:25
  427.3 22.0 %collective-permute-start.9 = (f32[1,4,64,256]{3,2,1,0:T(8,128)S(1)}, f32[1,4,64,256]{3,2,1,0:T(8,128)S(1)}, u32[]{:S(2)}, u32[]{:S(2)}) collective-permute-start(f32[1,4,64,256]{3,2,1,0:T(8,128)S(1)} %get-tuple-element.199), channel_id=1, source_target_pairs={{0,96},{16,112},{32,64},{48,80},{64,32},{80,48},{96,0},{112,16},{1... | collective-permute-start | bytes 786440 | tf_op jit(solution)/shard_map/ppermute | solution.py:25
  431.1 22.1 %collective-permute-start.10 = (f32[1,4,64,256]{3,2,1,0:T(8,128)S(1)}, f32[1,4,64,256]{3,2,1,0:T(8,128)S(1)}, u32[]{:S(2)}, u32[]{:S(2)}) collective-permute-start(f32[1,4,64,256]{3,2,1,0:T(8,128)S(1)} %get-tuple-element.198), channel_id=1, source_target_pairs={{0,112},{16,96},{32,80},{48,64},{64,48},{80,32},{96,16},{112,0},{1... | collective-permute-start | bytes 786440 | tf_op jit(solution)/shard_map/ppermute | solution.py:25
  453.2 1.3 copy-start.3
